TPU v7x, 128 devices: a whole 4x4x4 slice. The times are simulated.
128 devices in a mesh: row: 16 (over z_lo, y, core), col: 8 (over z_hi, x).
Axes of the slice: x: 4, y: 4, z: 4 (z_hi: 2, z_lo: 2; z = z_hi * 2 + z_lo), core: 2. Of those that a mesh axis runs over, the one named last changes fastest.
Arguments:
- a_tiles: bfloat16 [2048, 32, 64, 64], P('row', 'col'), may hold values from -6 to 6
- a_cols: int32 [2048, 32], P('row', 'col'), may hold values from 0 to 2047, as said below
- p_tiles: bfloat16 [2048, 64, 64], P(('col', 'row')), may hold values from -0.75 to 0.75
- agg_sizes: int32 [16, 16], P('row'), may hold values from 1 to 24, 128 in all within a row
Outputs:
- coarse: float32 [256, 64, 16384], P(None, None, ('col', 'row'))
Inputs may be any that keep to these rules, and one draw needn't show every extreme that they name: a_cols[i, s] is a fine block of column group s // 4: from (s // 4) * 256 to (s // 4 + 1) * 256 - 1.
All inputs are finite; a program needn't handle non-finite values.
Results may differ from a plain program's by a relative error of at most 0.0029.
Values may be sent and summed in bfloat16 or wider, within the bound.
A program may use at most 192 MiB of HBM per device.

v0:
```python
import jax
import jax.numpy as jnp
from jax import lax
from jax.experimental import pallas as pl
from jax.experimental.pallas import tpu as pltpu
from jax.sharding import PartitionSpec as P

MESH = pl.DeviceIdType.MESH
ROWS = 16
COLS = 8
MIB = 1 << 20
PITCH = 136
TILES = 512
GROUP = 8
BF = jnp.bfloat16
F32 = jnp.float32
I32 = jnp.int32

ORDER = [
    (0, 1, 0), (0, 3, 0), (1, 0, 0), (1, 2, 0), (0, 2, 0), (1, 1, 0), (1, 3, 0),
    (0, 1, 1), (0, 3, 1), (1, 0, 1), (1, 2, 1), (0, 2, 1), (1, 1, 1), (1, 3, 1), (0, 0, 1),
]


def place(zl, y, core, zh, x):
    return (zl * 8 + y * 2 + core, zh * 4 + x)


def iota(shape, dim):
    return lax.broadcasted_iota(I32, shape, dim).astype(F32)


def to_column(row):
    eye = iota((128, 128), 0) == iota((128, 128), 1)
    return jnp.sum(jnp.where(eye, row, 0.0), axis=1, keepdims=True)


def ranks_of(sizes):
    column = to_column(sizes)[:16]
    ahead = jnp.logical_or(
        column < sizes,
        jnp.logical_and(column == sizes, iota((16, 128), 0) < iota((16, 128), 1)),
    )
    return jnp.sum(jnp.where(ahead, 1.0, 0.0), axis=0, keepdims=True)


def ends_column(sizes):
    upto = iota((16, 128), 1) <= iota((16, 128), 0)
    return jnp.sum(jnp.where(upto, sizes, 0.0), axis=1, keepdims=True)


def aggregates(sizes):
    ends = ends_column(sizes)
    return jnp.sum(jnp.where(ends <= iota((16, 128), 1), 1.0, 0.0), axis=0, keepdims=True)


def plan(own_sizes, low_sizes, high_sizes, local_cols):
    owner = aggregates(own_sizes)
    rank_column = to_column(ranks_of(own_sizes))[:16]
    row_rank = jnp.sum(
        jnp.where(iota((16, 128), 0) == owner, rank_column, 0.0), axis=0, keepdims=True
    )
    low, high = aggregates(low_sizes), aggregates(high_sizes) + 16.0
    low_column, high_column = to_column(low), to_column(high)
    codes = []
    for s in range(4):
        j = local_cols[s]
        target = jnp.sum(
            jnp.where(iota((128, 128), 0) == j, low_column, 0.0)
            + jnp.where(iota((128, 128), 0) + 128.0 == j, high_column, 0.0),
            axis=0, keepdims=True,
        )
        key = row_rank * 32.0 + target
        codes.append(key * 512.0 + (iota((1, 128), 1) + 128.0 * s))
    columns = [to_column(code) for code in codes]
    places = []
    for s in range(4):
        places.append(sum(
            jnp.sum(jnp.where(column < codes[s], 1.0, 0.0), axis=0, keepdims=True)
            for column in columns
        ))
    place_columns = [to_column(p) for p in places]
    order, last = [], []
    for s in range(4):
        n = iota((128, 128), 1) + 128.0 * s
        order.append(sum(
            jnp.sum(jnp.where(place_columns[q] == n, columns[q], 0.0), axis=0, keepdims=True)
            for q in range(4)
        ))
        upto = [
            sum(
                jnp.sum(jnp.where(column < (n + extra) * 512.0, 1.0, 0.0), axis=0, keepdims=True)
                for column in columns
            )
            for extra in (0.0, 1.0)
        ]
        last.append(jnp.where(upto[1] > upto[0], upto[1] - 1.0, float(TILES)))
    return order, last, [low, high]


def fused_kernel(p_hbm, s_hbm, cols_hbm, a_hbm, got, ranks_out,
                 p_in, s_in, cols_v, cols_s, sizes, mine, col_p, row_p, a_in, mid,
                 table, left, seq, running, parts, meta_v, meta_s, ranks_v,
                 in_sem, send_sem, col_sem, row_sem, size_send, size_sem, local_sem, a_sem,
                 meta_sem, part_send, part_sem):
    row = lax.axis_index("row")
    col = lax.axis_index("col")
    zl, y, core = row // 8, (row // 2) % 4, row % 2
    zh, x = col // 4, col % 4

    sibling = place(zl, y, 1 - core, zh, x)
    partner = place(1 - zl, y, core, zh, x)
    along_y = [place(zl, (y + d) % 4, core, zh, x) for d in (1, 3, 2)]
    across = place(zl, y, core, 1 - zh, x)
    along_x = [place(zl, y, core, zh, (x + d) % 4) for d in (1, 3, 2)]
    peers = [place((zl + a) % 2, (y + b) % 4, (core + c) % 2, zh, x) for a, b, c in ORDER]
    to = place(zh, x, zl, core, y)
    source = place(core, x, zh, zl, y)
    stays = jnp.logical_and(to[0] == row, to[1] == col)
    moves = jnp.logical_not(stays)

    inputs = [
        pltpu.make_async_copy(s_hbm, s_in, in_sem.at[0]),
        pltpu.make_async_copy(p_hbm, p_in, in_sem.at[1]),
        pltpu.make_async_copy(cols_hbm, cols_v, in_sem.at[2]),
        pltpu.make_async_copy(cols_hbm, cols_s, in_sem.at[3]),
    ]
    for copy in inputs:
        copy.start()

    def a_copy(k):
        return pltpu.make_async_copy(
            a_hbm.at[:, pl.ds(8 * k, 8)], a_in.at[:, pl.ds(8 * k, 8)], a_sem.at[k]
        )

    for k in range(8):
        a_copy(k).start()

    barrier = pltpu.get_barrier_semaphore()
    for there in [*peers, across, *along_x]:
        pl.semaphore_signal(barrier, 1, device_id=there, device_id_type=MESH)

    @pl.when(moves)
    def _():
        pl.semaphore_signal(barrier, 1, device_id=source, device_id_type=MESH)

    inputs[0].wait()
    s_row = jnp.zeros((8, 128), I32)
    sizes[pl.ds(row, 1)] = s_row[None]
    sizes[row, 0:1, 0:16] = s_in[...]
    inputs[1].wait()
    for k in range(8):
        mine[pl.ds(64 * k, 64), :] = jnp.concatenate([p_in[2 * k], p_in[2 * k + 1]], axis=-1)

    pl.semaphore_wait(barrier, 19 + jnp.where(stays, 0, 1))

    count = [0]
    sent = []

    def send(src, dst, sem, there):
        k = count[0]
        count[0] += 1
        copy = pltpu.make_async_remote_copy(
            src_ref=src, dst_ref=dst, send_sem=send_sem.at[k], recv_sem=sem,
            device_id=there, device_id_type=MESH,
        )
        copy.start()
        sent.append(copy)

    def arrived(ref, sem):
        pltpu.make_async_copy(ref, ref, sem).wait()

    def row_of(a, b, c):
        return a * 8 + b * 2 + c

    held = 2 * x + zh
    first = pltpu.make_async_remote_copy(
        src_ref=mine, dst_ref=row_p.at[2 * y + core],
        send_sem=send_sem.at[24], recv_sem=row_sem.at[2 * y + core],
        device_id=to, device_id_type=MESH,
    )
    first_here = pltpu.make_async_copy(mine, row_p.at[2 * y + core], row_sem.at[2 * y + core])

    @pl.when(moves)
    def _():
        first.start()

    @pl.when(stays)
    def _():
        first_here.start()

    for there in peers:
        pltpu.make_async_remote_copy(
            src_ref=sizes.at[row], dst_ref=sizes.at[row], send_sem=size_send, recv_sem=size_sem,
            device_id=there, device_id_type=MESH,
        ).start()

    for there in [partner, *along_y, sibling]:
        send(mine, col_p.at[row], col_sem.at[row], there)
    own = pltpu.make_async_copy(mine, col_p.at[row], local_sem)
    own.start()

    eye = (iota((128, 128), 0) == iota((128, 128), 1)).astype(BF)

    def turn(k):
        a_copy(k).wait()

        @pl.loop(0, 8, unroll=2)
        def _(n):
            u = 8 * k + n
            wide = jnp.concatenate([a_in[s, u] for s in range(4)], axis=0)
            tiles = lax.dot_general(eye, wide, (((1,), (1,)), ((), ())), preferred_element_type=F32)
            for h in range(2):
                at = pl.multiple_of(PITCH * (64 * h + u), 8)
                mid[pl.ds(at, 128), :] = tiles[:, 128 * h:128 * h + 128]

    lane = lax.broadcasted_iota(I32, (64, 128), 1) // 64
    zero = jnp.zeros((64, 128), BF)

    def tabulate(src):
        @pl.loop(0, 8, unroll=4)
        def _(k):
            pair = col_p[src, pl.ds(pl.multiple_of(64 * k, 64), 64), :]
            turned = jnp.concatenate([pair[:, 64:], pair[:, :64]], axis=-1)
            for h in range(2):
                j = 16 * src + 2 * k + h
                right = meta_s[8 + (j >> 7), j & 127] & 1
                table[j] = jnp.where(lane == right, jnp.where(right == h, pair, turned), zero)

    def flip(slot):
        @pl.loop(0, 8, unroll=4)
        def _(k):
            pair = row_p[slot, pl.ds(pl.multiple_of(64 * k, 64), 64), :].T
            left[16 * slot + 2 * k] = pair[:64]
            left[16 * slot + 2 * k + 1] = pair[64:]

    turn(0)

    inputs[2].wait()
    inputs[3].wait()
    pltpu.make_async_copy(sizes.at[pl.ds(0, 15)], sizes.at[pl.ds(0, 15)], size_sem).wait()
    pltpu.make_async_copy(sizes.at[pl.ds(0, 15)], sizes.at[pl.ds(0, 15)], size_send).wait()

    def sizes_of(index):
        return sizes[index, 0:1, :].astype(F32)

    order, last, halves = plan(
        sizes_of(row), sizes_of(2 * col), sizes_of(2 * col + 1),
        [(cols_v[s:s + 1, :] & 255).astype(F32) for s in range(4)],
    )
    for k in range(4):
        meta_v[k:k + 1, :] = order[k].astype(I32)
        meta_v[4 + k:5 + k, :] = last[k].astype(I32)
    for k in range(2):
        meta_v[8 + k:9 + k, :] = halves[k].astype(I32)
    to_scalars = pltpu.make_async_copy(meta_v, meta_s, meta_sem)
    to_scalars.start()

    other = row_of(1 - zl, y, core)
    arrived(col_p.at[other], col_sem.at[other])
    for there in [*along_y, sibling]:
        send(col_p.at[other], col_p.at[other], col_sem.at[other], there)
    arrived(row_p.at[held], row_sem.at[held])
    for there in [across, *along_x]:
        send(row_p.at[held], row_p.at[held], row_sem.at[held], there)

    turn(1)
    turn(2)

    across_held = 2 * x + 1 - zh
    arrived(row_p.at[across_held], row_sem.at[across_held])
    for there in along_x:
        send(row_p.at[across_held], row_p.at[across_held], row_sem.at[across_held], there)

    turn(3)
    turn(4)
    to_scalars.wait()
    own.wait()
    tabulate(row)
    tabulate(other)
    for a, h in ((zl, 0), (1 - zl, 1)):
        for d in (1, 3, 2):
            index = row_of(a, (y + d) % 4, core)
            arrived(col_p.at[index], col_sem.at[index])
            send(col_p.at[index], col_p.at[index], col_sem.at[index], sibling)
        turn(5 + h)
    turn(7)
    flip(held)
    flip(across_held)
    for a in (zl, 1 - zl):
        for d in (1, 3, 2):
            tabulate(row_of(a, (y + d) % 4, core))
    for d in (1, 3, 2):
        for h in (0, 1):
            index = 2 * ((x + d) % 4) + h
            arrived(row_p.at[index], row_sem.at[index])
            flip(index)

    @pl.loop(0, ROWS)
    def _(k):
        ranks_v[pl.ds(k, 1), :] = ranks_of(sizes_of(k)).astype(I32)

    ranks_copy = pltpu.make_async_copy(ranks_v, ranks_out, local_sem)
    ranks_copy.start()
    for a in (zl, 1 - zl):
        for d in (0, 1, 3, 2):
            index = row_of(a, (y + d) % 4, 1 - core)
            arrived(col_p.at[index], col_sem.at[index])
            tabulate(index)

    seq[TILES] = zero
    running[...] = jnp.zeros((64, 128), F32)

    def exchange_copy(there, q):
        return pltpu.make_async_remote_copy(
            src_ref=parts.at[there[0], pl.ds(2 * q, 2)],
            dst_ref=got.at[row, pl.ds(2 * q, 2)],
            send_sem=part_send.at[there[0]],
            recv_sem=part_sem.at[row],
            device_id=there,
            device_id_type=MESH,
        )

    @pl.loop(0, 8)
    def _(q):
        @pl.loop(0, 64 // GROUP)
        def _(m):
            start = 64 * q + GROUP * m
            before = jnp.maximum(start - 1, 0)
            previous = jnp.where(start == 0, -1, meta_s[before >> 7, before & 127] >> 9)
            rows, products, keeps = [], [], []
            for g in range(GROUP):
                n = start + g
                code = meta_s[n >> 7, n & 127]
                key = code >> 9
                keeps.append(key == previous)
                previous = key
                s = (code >> 7) & 3
                i = code & 127
                rows.append(i)
                j = cols_s[s, i] & 255
                tile = mid[pl.ds((s >> 1) * (64 * PITCH) + i, 64, stride=PITCH), :]
                tile = jnp.where(lane == (s & 1), tile, 0.0).astype(BF)
                right = table[j]
                products.append(
                    jnp.dot(
                        tile, jnp.concatenate([right, right], axis=0), preferred_element_type=F32
                    ).astype(BF)
                )
            pieces = [
                jnp.dot(left[rows[g]], products[g], preferred_element_type=F32)
                for g in range(GROUP)
            ]
            total = running[...]
            for g in range(GROUP):
                total = pieces[g] + jnp.where(keeps[g], total, 0.0)
                seq[start + g] = total.astype(BF)
            running[...] = total

        @pl.loop(0, ROWS, unroll=2)
        def _(d):
            for h in range(2):
                key = (2 * q + h) * 32 + 2 * d
                one = jnp.clip(meta_s[4 + (key >> 7), key & 127], 0, TILES)
                two = jnp.clip(meta_s[4 + (key >> 7), (key & 127) + 1], 0, TILES)
                parts[d, 2 * q + h] = jnp.where(lane == 0, seq[one], seq[two])

        for there in peers:
            exchange_copy(there, q).start()

    mine_copy = pltpu.make_async_copy(parts.at[row], got.at[row], part_send.at[row])
    mine_copy.start()

    @pl.when(moves)
    def _():
        first.wait_send()

    for copy in sent:
        copy.wait_send()
    ranks_copy.wait()
    mine_copy.wait()
    for there in peers:
        arrived(parts.at[there[0]], part_send.at[there[0]])
        arrived(got.at[there[0]], part_sem.at[there[0]])


def fused(p_tiles, sizes, a_cols, a_turned):
    hbm = pl.BlockSpec(memory_space=pltpu.HBM)
    free = pl.BlockSpec(memory_space=pl.ANY)
    dma = pltpu.SemaphoreType.DMA
    return pl.pallas_call(
        fused_kernel,
        out_shape=(
            jax.ShapeDtypeStruct((ROWS, 16, 64, 128), BF),
            jax.ShapeDtypeStruct((ROWS, 128), I32),
        ),
        in_specs=[hbm] * 4,
        out_specs=[free, free],
        scratch_shapes=[
            pltpu.VMEM((16, 64, 64), BF),
            pltpu.VMEM((1, 16), I32),
            pltpu.VMEM((4, 128), I32),
            pltpu.SMEM((4, 128), I32),
            pltpu.VMEM((ROWS, 8, 128), I32),
            pltpu.VMEM((512, 128), BF),
            pltpu.VMEM((ROWS, 512, 128), BF),
            pltpu.VMEM((8, 512, 128), BF),
            pltpu.VMEM((4, 64, 64, 128), BF),
            pltpu.VMEM((128 * PITCH, 128), F32),
            pltpu.VMEM((256, 64, 128), BF),
            pltpu.VMEM((128, 64, 64), BF),
            pltpu.VMEM((TILES + 1, 64, 128), BF),
            pltpu.VMEM((64, 128), F32),
            pltpu.VMEM((ROWS, 16, 64, 128), BF),
            pltpu.VMEM((16, 128), I32),
            pltpu.SMEM((16, 128), I32),
            pltpu.VMEM((ROWS, 128), I32),
            dma((4,)),
            dma((25,)),
            dma((ROWS,)),
            dma((8,)),
            dma,
            dma,
            dma,
            dma((8,)),
            dma,
            dma((ROWS,)),
            dma((ROWS,)),
        ],
        compiler_params=pltpu.CompilerParams(
            collective_id=0, has_side_effects=True, vmem_limit_bytes=48 * MIB
        ),
    )(p_tiles, sizes, a_cols, a_turned)


def widen_kernel(ranks, got, out_hbm, wide, sem):
    def copy(k):
        return pltpu.make_async_copy(wide.at[k % 4], out_hbm.at[pl.ds(16 * k, 16)], sem.at[k % 4])

    for k in range(ROWS):
        if k >= 4:
            copy(k - 4).wait()

        @pl.loop(0, 16, unroll=2)
        def _(a):
            wide[k % 4, a] = got[k, ranks[k, a]].astype(F32)

        copy(k).start()
    for k in range(ROWS - 4, ROWS):
        copy(k).wait()


def widen(ranks, got):
    return pl.pallas_call(
        widen_kernel,
        out_shape=jax.ShapeDtypeStruct((256, 64, 128), F32),
        in_specs=[
            pl.BlockSpec(memory_space=pltpu.SMEM),
            pl.BlockSpec(memory_space=pltpu.VMEM),
        ],
        out_specs=pl.BlockSpec(memory_space=pltpu.HBM),
        scratch_shapes=[pltpu.VMEM((4, 16, 64, 128), F32), pltpu.SemaphoreType.DMA((4,))],
        compiler_params=pltpu.CompilerParams(vmem_limit_bytes=12 * MIB),
    )(ranks, got)


def per_device(a_tiles, a_cols, p_tiles, agg_sizes):
    got, ranks = fused(p_tiles, agg_sizes, a_cols.T, a_tiles.transpose(1, 2, 3, 0))
    return widen(ranks, got)


def solution(mesh):
    return jax.shard_map(
        per_device,
        mesh=mesh,
        in_specs=(
            P("row", "col", None, None),
            P("row", "col"),
            P(("col", "row"), None, None),
            P("row", None),
        ),
        out_specs=P(None, None, ("col", "row")),
        check_vma=False,
    )
```

profile of v0, /device:TPU:1, one launch (start us, length us, event | category | flops | bytes accessed | tf_op | source)
XLA Modules:
  0.0 92.8 jit_solution(10859439422100729459)
XLA Ops:
  0.0 0.0 copy-start
  0.0 0.9 %copy-done = bf16[16,64,64]{2,1,0:T(8,128)(2,1)S(1)} copy-done((bf16[16,64,64]{2,1,0:T(8,128)(2,1)S(1)}, bf16[16,64,64]{2,1,0:T(8,128)(2,1)}, u32[]{:S(2)}) %copy-start) | copy-done | bytes 131096
  1.0 0.0 copy-start.1
  1.0 0.7 copy-done.1
  1.6 0.0 copy-start.2
  1.6 0.7 copy-done.2
  2.3 85.8 %shard_map.46 = (bf16[16,16,64,128]{3,2,1,0:T(8,128)(2,1)S(1)}, s32[16,128]{1,0:T(8,128)S(1)}) custom-call(bf16[16,64,64]{2,1,0:T(8,128)(2,1)S(1)} %copy-done, s32[1,16]{1,0:T(1,128)S(1)} %copy-done.2, s32[4,128]{1,0:T(4,128)S(1)} %bitcast.2, bf16[4,64,64,128]{3,2,1,0:T(8,128)(2,1)} %bitcast.3), custom_call_target="tpu_custom_call" | custom-call | tf_op jit(solution)/shard_map/pallas_call | solution.py:391
  88.1 4.7 %shard_map.47 = f32[256,64,128]{2,1,0:T(8,128)} custom-call(s32[16,128]{1,0:T(8,128)S(1)} %get-tuple-element.7.ranks, bf16[16,16,64,128]{3,2,1,0:T(8,128)(2,1)S(1)} %get-tuple-element.8.got), custom_call_target="tpu_custom_call" | custom-call | tf_op jit(solution)/shard_map/pallas_call | solution.py:454
Async XLA Ops:
  0.0 0.9 %copy-start = (bf16[16,64,64]{2,1,0:T(8,128)(2,1)S(1)}, bf16[16,64,64]{2,1,0:T(8,128)(2,1)}, u32[]{:S(2)}) copy-start(bf16[16,64,64]{2,1,0:T(8,128)(2,1)} %p_hbm.1) | copy-start | bytes 393220
  1.0 0.7 copy-start.1
  1.6 0.7 copy-start.2
where the time goes:
time: 93 us; the launch traced here: 92.8 us
  Pallas kernels  90.6 us (97%)
  local copies, waits for them, and re-layouts  2.29 us (2%)
    pallas_call x1, Pallas kernels, fused(): pl.pallas_call(fused_kernel, out_shape=(jax.ShapeDtypeStruct((ROWS, 16, 6...  85.8 us
    pallas_call x1, Pallas kernels, widen(): pl.pallas_call(widen_kernel, out_shape=jax.ShapeDtypeStruct((256, 64, 128...  4.72 us
    unnamed x6, local copies, waits for them, and re-layouts  2.29 us

commit v1 on v0

v1 whole, which is shorter than its diff:
```python
import jax
import jax.numpy as jnp
from jax import lax
from jax.experimental import pallas as pl
from jax.experimental.pallas import tpu as pltpu
from jax.sharding import PartitionSpec as P

MESH = pl.DeviceIdType.MESH
ROWS = 16
COLS = 8
MIB = 1 << 20
PITCH = 136
TILES = 512
GROUP = 16
BF = jnp.bfloat16
F32 = jnp.float32
I32 = jnp.int32

ORDER = [
    (0, 1, 0), (0, 3, 0), (1, 0, 0), (1, 2, 0), (0, 2, 0), (1, 1, 0), (1, 3, 0),
    (0, 1, 1), (0, 3, 1), (1, 0, 1), (1, 2, 1), (0, 2, 1), (1, 1, 1), (1, 3, 1), (0, 0, 1),
]


def place(zl, y, core, zh, x):
    return (zl * 8 + y * 2 + core, zh * 4 + x)


def iota(shape, dim):
    return lax.broadcasted_iota(I32, shape, dim).astype(F32)


def to_column(row):
    eye = iota((128, 128), 0) == iota((128, 128), 1)
    return jnp.sum(jnp.where(eye, row, 0.0), axis=1, keepdims=True)


def ranks_of(sizes):
    column = to_column(sizes)[:16]
    ahead = jnp.logical_or(
        column < sizes,
        jnp.logical_and(column == sizes, iota((16, 128), 0) < iota((16, 128), 1)),
    )
    return jnp.sum(jnp.where(ahead, 1.0, 0.0), axis=0, keepdims=True)


def ends_column(sizes):
    upto = iota((16, 128), 1) <= iota((16, 128), 0)
    return jnp.sum(jnp.where(upto, sizes, 0.0), axis=1, keepdims=True)


def aggregates(sizes):
    ends = ends_column(sizes)
    return jnp.sum(jnp.where(ends <= iota((16, 128), 1), 1.0, 0.0), axis=0, keepdims=True)


def plan(own_sizes, low_sizes, high_sizes, local_cols):
    owner = aggregates(own_sizes)
    rank_column = to_column(ranks_of(own_sizes))[:16]
    row_rank = jnp.sum(
        jnp.where(iota((16, 128), 0) == owner, rank_column, 0.0), axis=0, keepdims=True
    )
    low, high = aggregates(low_sizes), aggregates(high_sizes) + 16.0
    low_column, high_column = to_column(low), to_column(high)
    codes = []
    for s in range(4):
        j = local_cols[s]
        target = jnp.sum(
            jnp.where(iota((128, 128), 0) == j, low_column, 0.0)
            + jnp.where(iota((128, 128), 0) + 128.0 == j, high_column, 0.0),
            axis=0, keepdims=True,
        )
        key = row_rank * 32.0 + target
        codes.append(key * 512.0 + (iota((1, 128), 1) + 128.0 * s))
    columns = [to_column(code) for code in codes]
    places = []
    for s in range(4):
        places.append(sum(
            jnp.sum(jnp.where(column < codes[s], 1.0, 0.0), axis=0, keepdims=True)
            for column in columns
        ))
    place_columns = [to_column(p) for p in places]
    order, last = [], []
    for s in range(4):
        n = iota((128, 128), 1) + 128.0 * s
        order.append(sum(
            jnp.sum(jnp.where(place_columns[q] == n, columns[q], 0.0), axis=0, keepdims=True)
            for q in range(4)
        ))
        upto = [
            sum(
                jnp.sum(jnp.where(column < (n + extra) * 512.0, 1.0, 0.0), axis=0, keepdims=True)
                for column in columns
            )
            for extra in (0.0, 1.0)
        ]
        last.append(jnp.where(upto[1] > upto[0], upto[1] - 1.0, float(TILES)))
    return order, last, [low, high]


def fused_kernel(p_hbm, s_hbm, cols_hbm, a_hbm, got, ranks_out,
                 p_in, s_in, cols_v, cols_s, sizes, mine, mine_left, col_p, row_p, a_in, mid, a_buf,
                 table, left, products, seq, running, parts, meta_v, meta_s, ranks_v,
                 in_sem, send_sem, col_sem, row_sem, first_sem, size_send, size_sem, local_sem, a_sem,
                 meta_sem, part_send, part_sem):
    row = lax.axis_index("row")
    col = lax.axis_index("col")
    zl, y, core = row // 8, (row // 2) % 4, row % 2
    zh, x = col // 4, col % 4

    sibling = place(zl, y, 1 - core, zh, x)
    partner = place(1 - zl, y, core, zh, x)
    along_y = [place(zl, (y + d) % 4, core, zh, x) for d in (1, 3)]
    across = place(zl, y, core, 1 - zh, x)
    along_x = [place(zl, y, core, zh, (x + d) % 4) for d in (1, 3)]
    peers = [place((zl + a) % 2, (y + b) % 4, (core + c) % 2, zh, x) for a, b, c in ORDER]
    to = place(zh, x, zl, core, (x + y) % 4)
    source = place(core, (x - y + 4) % 4, zh, zl, y)
    stays = jnp.logical_and(to[0] == row, to[1] == col)
    moves = jnp.logical_not(stays)

    inputs = [
        pltpu.make_async_copy(s_hbm, s_in, in_sem.at[0]),
        pltpu.make_async_copy(p_hbm, p_in, in_sem.at[1]),
        pltpu.make_async_copy(cols_hbm, cols_v, in_sem.at[2]),
        pltpu.make_async_copy(cols_hbm, cols_s, in_sem.at[3]),
    ]
    for copy in inputs:
        copy.start()

    def a_copy(k):
        return pltpu.make_async_copy(
            a_hbm.at[:, pl.ds(8 * k, 8)], a_in.at[:, pl.ds(8 * k, 8)], a_sem.at[k]
        )

    for k in range(8):
        a_copy(k).start()

    barrier = pltpu.get_barrier_semaphore()
    for there in [*peers, across, *along_x]:
        pl.semaphore_signal(barrier, 1, device_id=there, device_id_type=MESH)

    @pl.when(moves)
    def _():
        pl.semaphore_signal(barrier, 1, device_id=source, device_id_type=MESH)

    inputs[0].wait()
    s_row = jnp.zeros((8, 128), I32)
    sizes[pl.ds(row, 1)] = s_row[None]
    sizes[row, 0:1, 0:16] = s_in[...]
    inputs[1].wait()
    for k in range(8):
        mine[pl.ds(64 * k, 64), :] = jnp.concatenate([p_in[2 * k], p_in[2 * k + 1]], axis=-1)
    for h in range(2):
        for k in range(4):
            mine_left[h, pl.ds(64 * k, 64), :] = jnp.concatenate(
                [p_in[4 * k + n][:, 32 * h:32 * h + 32] for n in range(4)], axis=-1
            )

    pl.semaphore_wait(barrier, 18 + jnp.where(stays, 0, 1))

    count = [0]
    sent = []

    def send(src, dst, sem, there):
        k = count[0]
        count[0] += 1
        copy = pltpu.make_async_remote_copy(
            src_ref=src, dst_ref=dst, send_sem=send_sem.at[k], recv_sem=sem,
            device_id=there, device_id_type=MESH,
        )
        copy.start()
        sent.append(copy)

    def arrived(ref, sem):
        pltpu.make_async_copy(ref, ref, sem).wait()

    def row_of(a, b, c):
        return a * 8 + b * 2 + c

    def slot_at(x, h):
        return 2 * ((x - y + 4) % 4) + h

    held, across_held = slot_at(x, zh), slot_at(x, 1 - zh)

    def first(u):
        return pltpu.make_async_remote_copy(
            src_ref=mine_left.at[u], dst_ref=row_p.at[u, 2 * y + core],
            send_sem=first_sem.at[u], recv_sem=row_sem.at[u, 2 * y + core],
            device_id=to, device_id_type=MESH,
        )

    def first_step(u):
        @pl.when(moves)
        def _():
            first(u).start()

        @pl.when(stays)
        def _():
            pltpu.make_async_copy(
                mine_left.at[u], row_p.at[u, 2 * y + core], row_sem.at[u, 2 * y + core]
            ).start()

    first_step(0)

    for there in peers:
        pltpu.make_async_remote_copy(
            src_ref=sizes.at[row], dst_ref=sizes.at[row], send_sem=size_send, recv_sem=size_sem,
            device_id=there, device_id_type=MESH,
        ).start()

    def col_send(index, there, half=None):
        rows = pl.ds(0, 512) if half is None else pl.ds(256 * half, 256)
        ref = col_p.at[index, rows]
        send(mine if index is row else ref, ref, col_sem.at[index], there)

    def row_send(u, slot, there, half=None):
        rows = pl.ds(0, 256) if half is None else pl.ds(128 * half, 128)
        ref = row_p.at[u, slot, rows]
        send(ref, ref, row_sem.at[u, slot], there)

    def row_arrived(u, slot):
        arrived(row_p.at[u, slot], row_sem.at[u, slot])

    right_y, left_y = along_y
    right_x, left_x = along_x
    for there in (partner, right_y, left_y, sibling):
        col_send(row, there)
    own = pltpu.make_async_copy(mine, col_p.at[row], local_sem)
    own.start()

    def turn(k):
        a_copy(k).wait()

        @pl.loop(0, 8, unroll=2)
        def _(n):
            u = 8 * k + n
            wide = jnp.concatenate([a_in[s, u] for s in range(4)], axis=0)
            tiles = wide.T.astype(F32)
            for h in range(2):
                at = pl.multiple_of(PITCH * (64 * h + u), 8)
                mid[pl.ds(at, 128), :] = tiles[:, 128 * h:128 * h + 128]

    def pick(k):
        @pl.loop(0, 16, unroll=4)
        def _(n):
            i = 16 * k + n
            for h in range(2):
                both = mid[pl.ds(64 * PITCH * h + i, 64, stride=PITCH), :]
                a_buf[256 * h + i] = both[:, :64].astype(BF)
                a_buf[256 * h + 128 + i] = pltpu.roll(both, 64, 1)[:, :64].astype(BF)

    lane = lax.broadcasted_iota(I32, (64, 128), 1) // 64

    def flip(u, slot):
        for k in range(4):
            turned = row_p[u, slot, 64 * k:64 * k + 64, :].T
            for n in range(4):
                left[u, 16 * slot + 4 * k + n] = turned[32 * n:32 * n + 32]

    zero = jnp.zeros((64, 128), BF)

    def tabulate(src):
        @pl.loop(0, 8, unroll=4)
        def _(k):
            pair = col_p[src, pl.ds(pl.multiple_of(64 * k, 64), 64), :]
            turned = jnp.concatenate([pair[:, 64:], pair[:, :64]], axis=-1)
            for h in range(2):
                j = 16 * src + 2 * k + h
                right = meta_s[8 + (j >> 7), j & 127] & 1
                table[j] = jnp.where(lane == right, jnp.where(right == h, pair, turned), zero)

    turn(0)
    turn(1)

    row_arrived(0, held)
    row_send(0, held, right_x)
    row_send(0, held, left_x)
    row_send(0, held, across)
    other = row_of(1 - zl, y, core)
    arrived(col_p.at[other], col_sem.at[other])
    col_send(other, right_y)
    col_send(other, left_y)
    col_send(other, sibling)

    before_x, after_x = (x + 3) % 4, (x + 1) % 4
    before_y, after_y = (y + 3) % 4, (y + 1) % 4
    row_arrived(0, across_held)
    row_send(0, across_held, right_x)
    row_send(0, across_held, left_x)

    def row_relay(u, h):
        for where, half, there in ((before_x, 0, right_x), (after_x, 1, left_x)):
            row_arrived(u, slot_at(where, h))
            row_send(u, slot_at(where, h), there, half)

    def col_relay(a):
        for where, half, there in ((before_y, 0, right_y), (after_y, 1, left_y)):
            index = row_of(a, where, core)
            arrived(col_p.at[index], col_sem.at[index])
            col_send(index, there, half)
            col_send(index, sibling)

    for k in range(2, 6):
        turn(k)
    row_relay(0, zh)
    col_relay(zl)
    turn(6)
    turn(7)
    inputs[2].wait()
    inputs[3].wait()
    pltpu.make_async_copy(sizes.at[pl.ds(0, 15)], sizes.at[pl.ds(0, 15)], size_sem).wait()
    pltpu.make_async_copy(sizes.at[pl.ds(0, 15)], sizes.at[pl.ds(0, 15)], size_send).wait()

    def sizes_of(index):
        return sizes[index, 0:1, :].astype(F32)

    order, last, halves = plan(
        sizes_of(row), sizes_of(2 * col), sizes_of(2 * col + 1),
        [(cols_v[s:s + 1, :] & 255).astype(F32) for s in range(4)],
    )
    for k in range(4):
        meta_v[k:k + 1, :] = order[k].astype(I32)
        meta_v[4 + k:5 + k, :] = last[k].astype(I32)
    for k in range(2):
        meta_v[8 + k:9 + k, :] = halves[k].astype(I32)
    to_scalars = pltpu.make_async_copy(meta_v, meta_s, meta_sem)
    to_scalars.start()

    row_relay(0, 1 - zh)
    col_relay(1 - zl)
    first_step(1)
    pick(0)
    pick(1)
    for a in (zl, 1 - zl):
        index = row_of(a, (y + 2) % 4, core)
        arrived(col_p.at[index], col_sem.at[index])
        col_send(index, sibling)
    pick(2)
    pick(3)
    to_scalars.wait()
    own.wait()
    for slot in (held, across_held, *[slot_at(w, h) for w in (before_x, after_x) for h in (0, 1)]):
        flip(0, slot)
    for k in range(4, 8):
        pick(k)
    for a in (zl, 1 - zl):
        for d in range(4):
            tabulate(row_of(a, (y + d) % 4, core))

    for h in (zh, 1 - zh):
        slot = slot_at((x + 2) % 4, h)
        row_arrived(0, slot)
        flip(0, slot)
    for a in (zl, 1 - zl):
        for d in (0, 1, 3, 2):
            index = row_of(a, (y + d) % 4, 1 - core)
            arrived(col_p.at[index], col_sem.at[index])
            tabulate(index)

    seq[TILES] = jnp.zeros((32, 128), BF)
    running[...] = jnp.zeros((32, 128), F32)

    def exchange_copy(there, u, q):
        return pltpu.make_async_remote_copy(
            src_ref=parts.at[there[0], u, pl.ds(2 * q, 2)],
            dst_ref=got.at[row, u, pl.ds(2 * q, 2)],
            send_sem=part_send.at[there[0]],
            recv_sem=part_sem.at[row],
            device_id=there,
            device_id_type=MESH,
        )

    def chunks(u, begin, end):
        @pl.loop(begin, end)
        def _(q):
            @pl.loop(0, 64 // GROUP)
            def _(m):
                start = 64 * q + GROUP * m
                before = jnp.maximum(start - 1, 0)
                previous = jnp.where(start == 0, -1, meta_s[before >> 7, before & 127] >> 9)
                rows, keeps, rights = [], [], []
                for g in range(GROUP):
                    n = start + g
                    code = meta_s[n >> 7, n & 127]
                    key = code >> 9
                    keeps.append(key == previous)
                    previous = key
                    i = code & 127
                    rows.append(i)
                    if u == 0:
                        j = cols_s[(code >> 7) & 3, i] & 255
                        rights.append(
                            jnp.dot(
                                a_buf[code & 511], table[j], preferred_element_type=F32
                            ).astype(BF)
                        )
                        products[n] = rights[g]
                    else:
                        rights.append(products[n])
                pieces = [
                    jnp.dot(left[u, rows[g]], rights[g], preferred_element_type=F32)
                    for g in range(GROUP)
                ]
                total = running[...]
                for g in range(GROUP):
                    total = pieces[g] + jnp.where(keeps[g], total, 0.0)
                    seq[start + g] = total.astype(BF)
                running[...] = total

            @pl.loop(0, ROWS, unroll=4)
            def _(d):
                for h in range(2):
                    key = 64 * q + 32 * h + 2 * d
                    one = jnp.clip(meta_s[4 + (key >> 7), key & 127], 0, TILES)
                    two = jnp.clip(meta_s[4 + (key >> 7), (key & 127) + 1], 0, TILES)
                    parts[d, u, 2 * q + h] = jnp.where(lane[:32] == 0, seq[one], seq[two])

            for there in peers:
                exchange_copy(there, u, q).start()

    chunks(0, 0, 1)
    row_arrived(1, held)
    row_send(1, held, right_x)
    row_send(1, held, left_x)
    row_send(1, held, across)
    chunks(0, 1, 3)
    @pl.loop(0, ROWS)
    def _(k):
        ranks_v[pl.ds(k, 1), :] = ranks_of(sizes_of(k)).astype(I32)

    ranks_copy = pltpu.make_async_copy(ranks_v, ranks_out, local_sem)
    ranks_copy.start()
    row_arrived(1, across_held)
    row_send(1, across_held, right_x)
    row_send(1, across_held, left_x)
    row_relay(1, zh)
    chunks(0, 3, 5)
    row_relay(1, 1 - zh)
    chunks(0, 5, 8)
    for h in (zh, 1 - zh):
        row_arrived(1, slot_at((x + 2) % 4, h))
    for slot in range(8):
        flip(1, slot)
    chunks(1, 0, 8)

    mine_copy = pltpu.make_async_copy(parts.at[row], got.at[row], part_send.at[row])
    mine_copy.start()

    @pl.when(moves)
    def _():
        first(0).wait_send()
        first(1).wait_send()

    for copy in sent:
        copy.wait_send()
    ranks_copy.wait()
    mine_copy.wait()
    for there in peers:
        arrived(parts.at[there[0]], part_send.at[there[0]])
        arrived(got.at[there[0]], part_sem.at[there[0]])


def fused(p_tiles, sizes, a_cols, a_turned):
    hbm = pl.BlockSpec(memory_space=pltpu.HBM)
    free = pl.BlockSpec(memory_space=pl.ANY)
    dma = pltpu.SemaphoreType.DMA
    return pl.pallas_call(
        fused_kernel,
        out_shape=(
            jax.ShapeDtypeStruct((ROWS, 2, 16, 32, 128), BF),
            jax.ShapeDtypeStruct((ROWS, 128), I32),
        ),
        in_specs=[hbm] * 4,
        out_specs=[free, free],
        scratch_shapes=[
            pltpu.VMEM((16, 64, 64), BF),
            pltpu.VMEM((1, 16), I32),
            pltpu.VMEM((4, 128), I32),
            pltpu.SMEM((4, 128), I32),
            pltpu.VMEM((ROWS, 8, 128), I32),
            pltpu.VMEM((512, 128), BF),
            pltpu.VMEM((2, 256, 128), BF),
            pltpu.VMEM((ROWS, 512, 128), BF),
            pltpu.VMEM((2, 8, 256, 128), BF),
            pltpu.VMEM((4, 64, 64, 128), BF),
            pltpu.VMEM((128 * PITCH, 128), F32),
            pltpu.VMEM((TILES, 64, 64), BF),
            pltpu.VMEM((256, 64, 128), BF),
            pltpu.VMEM((2, 128, 32, 64), BF),
            pltpu.VMEM((TILES, 64, 128), BF),
            pltpu.VMEM((TILES + 1, 32, 128), BF),
            pltpu.VMEM((32, 128), F32),
            pltpu.VMEM((ROWS, 2, 16, 32, 128), BF),
            pltpu.VMEM((16, 128), I32),
            pltpu.SMEM((16, 128), I32),
            pltpu.VMEM((ROWS, 128), I32),
            dma((4,)),
            dma((35,)),
            dma((ROWS,)),
            dma((2, 8)),
            dma((2,)),
            dma,
            dma,
            dma,
            dma((8,)),
            dma,
            dma((ROWS,)),
            dma((ROWS,)),
        ],
        compiler_params=pltpu.CompilerParams(
            collective_id=0, has_side_effects=True, vmem_limit_bytes=58 * MIB
        ),
    )(p_tiles, sizes, a_cols, a_turned)


def widen_kernel(ranks_hbm, got, out_hbm, ranks, narrow, wide, ranks_sem, in_sem, sem):
    def fetch(k):
        return pltpu.make_async_copy(got.at[k], narrow.at[k], in_sem.at[k])

    def copy(k):
        return pltpu.make_async_copy(wide.at[k % 8], out_hbm.at[pl.ds(16 * k, 16)], sem.at[k % 8])

    ranks_copy = pltpu.make_async_copy(ranks_hbm, ranks, ranks_sem)
    ranks_copy.start()
    for k in range(ROWS):
        fetch(k).start()
    ranks_copy.wait()
    for k in range(ROWS):
        if k >= 8:
            copy(k - 8).wait()
        fetch(k).wait()

        @pl.loop(0, 16, unroll=4)
        def _(a):
            for h in range(2):
                wide[k % 8, a, 32 * h:32 * h + 32] = narrow[k, h, ranks[k, a]].astype(F32)

        copy(k).start()
    for k in range(ROWS - 8, ROWS):
        copy(k).wait()


def widen(ranks, got):
    free = pl.BlockSpec(memory_space=pl.ANY)
    return pl.pallas_call(
        widen_kernel,
        out_shape=jax.ShapeDtypeStruct((256, 64, 128), F32),
        in_specs=[free, free],
        out_specs=free,
        scratch_shapes=[
            pltpu.SMEM((ROWS, 128), I32),
            pltpu.VMEM((ROWS, 2, 16, 32, 128), BF),
            pltpu.VMEM((8, 16, 64, 128), F32),
            pltpu.SemaphoreType.DMA,
            pltpu.SemaphoreType.DMA((ROWS,)),
            pltpu.SemaphoreType.DMA((8,)),
        ],
        compiler_params=pltpu.CompilerParams(vmem_limit_bytes=58 * MIB),
    )(ranks, got)


def per_device(a_tiles, a_cols, p_tiles, agg_sizes):
    got, ranks = fused(p_tiles, agg_sizes, a_cols.T, a_tiles.transpose(1, 2, 3, 0))
    return widen(ranks, got)


def solution(mesh):
    return jax.shard_map(
        per_device,
        mesh=mesh,
        in_specs=(
            P("row", "col", None, None),
            P("row", "col"),
            P(("col", "row"), None, None),
            P("row", None),
        ),
        out_specs=P(None, None, ("col", "row")),
        check_vma=False,
    )
```

time: 93 us -> 86.7 us (0.932)
  Pallas kernels: 90.6 us -> 86.6 us
  local copies, waits for them, and re-layouts: 2.29 us -> 0 us
    pallas_call x1, Pallas kernels: 85.8 us -> 82.1 us  [fused(): pl.pallas_call(fused_kernel, out_shape=(jax.ShapeDtypeStruct((ROWS, 2, 16...]
    unnamed x6 -> x0, local copies, waits for them, and re-layouts: 2.29 us -> none
where the time goes in v1:
time: 86.7 us; the launch traced here: 86.6 us
  Pallas kernels  86.6 us (100%)
    pallas_call x1, Pallas kernels, fused(): pl.pallas_call(fused_kernel, out_shape=(jax.ShapeDtypeStruct((ROWS, 2, 16...  82.1 us
    pallas_call x1, Pallas kernels, widen(): pl.pallas_call(widen_kernel, out_shape=jax.ShapeDtypeStruct((256, 64, 128...  4.49 us

profile of v1, /device:TPU:1, one launch (start us, length us, event | category | flops | bytes accessed | tf_op | source)
XLA Modules:
  0.0 86.6 jit_solution(6260499004428010537)
XLA Ops:
  0.0 82.1 %shard_map.46 = (bf16[16,2,16,32,128]{4,3,2,1,0:T(8,128)(2,1)}, s32[16,128]{1,0:T(8,128)}) custom-call(bf16[16,64,64]{2,1,0:T(8,128)(2,1)} %p_hbm.1, s32[1,16]{1,0:T(1,128)} %s_hbm.1, s32[4,128]{1,0:T(4,128)} %bitcast.3, bf16[4,64,64,128]{3,2,1,0:T(8,128)(2,1)} %bitcast.2), custom_call_target="tpu_custom_call" | custom-call | tf_op jit(solution)/shard_map/pallas_call | solution.py:468
  82.1 4.5 %shard_map.47 = f32[256,64,128]{2,1,0:T(8,128)} custom-call(s32[16,128]{1,0:T(8,128)} %get-tuple-element.7.ranks_hbm, bf16[16,2,16,32,128]{4,3,2,1,0:T(8,128)(2,1)} %get-tuple-element.8.got), custom_call_target="tpu_custom_call" | custom-call | tf_op jit(solution)/shard_map/pallas_call | solution.py:546

commit v2 on v1

--- a/solution.py
+++ b/solution.py
@@ -60,8 +60,8 @@
     row_rank = jnp.sum(
         jnp.where(iota((16, 128), 0) == owner, rank_column, 0.0), axis=0, keepdims=True
     )
-    low, high = aggregates(low_sizes), aggregates(high_sizes) + 16.0
-    low_column, high_column = to_column(low), to_column(high)
+    low_column = to_column(aggregates(low_sizes))
+    high_column = to_column(aggregates(high_sizes) + 16.0)
     codes = []
     for s in range(4):
         j = local_cols[s]
@@ -70,7 +70,7 @@
             + jnp.where(iota((128, 128), 0) + 128.0 == j, high_column, 0.0),
             axis=0, keepdims=True,
         )
-        key = row_rank * 32.0 + target
+        key = row_rank * 64.0 + target * 2.0 + (j - 2.0 * jnp.floor(j * 0.5))
         codes.append(key * 512.0 + (iota((1, 128), 1) + 128.0 * s))
     columns = [to_column(code) for code in codes]
     places = []
@@ -87,20 +87,21 @@
             jnp.sum(jnp.where(place_columns[q] == n, columns[q], 0.0), axis=0, keepdims=True)
             for q in range(4)
         ))
-        upto = [
-            sum(
-                jnp.sum(jnp.where(column < (n + extra) * 512.0, 1.0, 0.0), axis=0, keepdims=True)
-                for column in columns
-            )
-            for extra in (0.0, 1.0)
+    key_columns = [jnp.floor(column * (1.0 / 512.0)) for column in columns]
+    for s in range(8):
+        n = iota((128, 128), 1) + 128.0 * s
+        at = [
+            jnp.max(jnp.where(key_columns[q] == n, place_columns[q], -1.0), axis=0, keepdims=True)
+            for q in range(4)
         ]
-        last.append(jnp.where(upto[1] > upto[0], upto[1] - 1.0, float(TILES)))
-    return order, last, [low, high]
+        at = jnp.maximum(jnp.maximum(at[0], at[1]), jnp.maximum(at[2], at[3]))
+        last.append(jnp.where(at < 0.0, float(TILES), at))
+    return order, last
 
 
 def fused_kernel(p_hbm, s_hbm, cols_hbm, a_hbm, got, ranks_out,
                  p_in, s_in, cols_v, cols_s, sizes, mine, mine_left, col_p, row_p, a_in, mid, a_buf,
-                 table, left, products, seq, running, parts, meta_v, meta_s, ranks_v,
+                 left, products, seq, running, parts, meta_v, meta_s, ranks_v,
                  in_sem, send_sem, col_sem, row_sem, first_sem, size_send, size_sem, local_sem, a_sem,
                  meta_sem, part_send, part_sem):
     row = lax.axis_index("row")
@@ -150,7 +151,7 @@
     sizes[row, 0:1, 0:16] = s_in[...]
     inputs[1].wait()
     for k in range(8):
-        mine[pl.ds(64 * k, 64), :] = jnp.concatenate([p_in[2 * k], p_in[2 * k + 1]], axis=-1)
+        mine[k] = jnp.concatenate([p_in[2 * k], p_in[2 * k + 1]], axis=-1)
     for h in range(2):
         for k in range(4):
             mine_left[h, pl.ds(64 * k, 64), :] = jnp.concatenate(
@@ -210,8 +211,8 @@
         ).start()
 
     def col_send(index, there, half=None):
-        rows = pl.ds(0, 512) if half is None else pl.ds(256 * half, 256)
-        ref = col_p.at[index, rows]
+        pairs = pl.ds(0, 8) if half is None else pl.ds(4 * half, 4)
+        ref = col_p.at[index, pairs]
         send(mine if index is row else ref, ref, col_sem.at[index], there)
 
     def row_send(u, slot, there, half=None):
@@ -257,18 +258,6 @@
             turned = row_p[u, slot, 64 * k:64 * k + 64, :].T
             for n in range(4):
                 left[u, 16 * slot + 4 * k + n] = turned[32 * n:32 * n + 32]
-
-    zero = jnp.zeros((64, 128), BF)
-
-    def tabulate(src):
-        @pl.loop(0, 8, unroll=4)
-        def _(k):
-            pair = col_p[src, pl.ds(pl.multiple_of(64 * k, 64), 64), :]
-            turned = jnp.concatenate([pair[:, 64:], pair[:, :64]], axis=-1)
-            for h in range(2):
-                j = 16 * src + 2 * k + h
-                right = meta_s[8 + (j >> 7), j & 127] & 1
-                table[j] = jnp.where(lane == right, jnp.where(right == h, pair, turned), zero)
 
     turn(0)
     turn(1)
@@ -315,15 +304,14 @@
     def sizes_of(index):
         return sizes[index, 0:1, :].astype(F32)
 
-    order, last, halves = plan(
+    order, last = plan(
         sizes_of(row), sizes_of(2 * col), sizes_of(2 * col + 1),
         [(cols_v[s:s + 1, :] & 255).astype(F32) for s in range(4)],
     )
     for k in range(4):
         meta_v[k:k + 1, :] = order[k].astype(I32)
+    for k in range(8):
         meta_v[4 + k:5 + k, :] = last[k].astype(I32)
-    for k in range(2):
-        meta_v[8 + k:9 + k, :] = halves[k].astype(I32)
     to_scalars = pltpu.make_async_copy(meta_v, meta_s, meta_sem)
     to_scalars.start()
 
@@ -344,10 +332,6 @@
         flip(0, slot)
     for k in range(4, 8):
         pick(k)
-    for a in (zl, 1 - zl):
-        for d in range(4):
-            tabulate(row_of(a, (y + d) % 4, core))
-
     for h in (zh, 1 - zh):
         slot = slot_at((x + 2) % 4, h)
         row_arrived(0, slot)
@@ -356,27 +340,26 @@
         for d in (0, 1, 3, 2):
             index = row_of(a, (y + d) % 4, 1 - core)
             arrived(col_p.at[index], col_sem.at[index])
-            tabulate(index)
-
-    seq[TILES] = jnp.zeros((32, 128), BF)
+
+    seq[TILES] = jnp.zeros((32, 128), F32)
     running[...] = jnp.zeros((32, 128), F32)
 
-    def exchange_copy(there, u, q):
+    def exchange_copy(there, u, ranks):
         return pltpu.make_async_remote_copy(
-            src_ref=parts.at[there[0], u, pl.ds(2 * q, 2)],
-            dst_ref=got.at[row, u, pl.ds(2 * q, 2)],
+            src_ref=parts.at[there[0], u, ranks],
+            dst_ref=got.at[row, u, ranks],
             send_sem=part_send.at[there[0]],
             recv_sem=part_sem.at[row],
             device_id=there,
             device_id_type=MESH,
         )
 
-    def chunks(u, begin, end):
+    def chunks(u, begin, end, width=2):
         @pl.loop(begin, end)
         def _(q):
-            @pl.loop(0, 64 // GROUP)
+            @pl.loop(0, 32 * width // GROUP)
             def _(m):
-                start = 64 * q + GROUP * m
+                start = 32 * width * q + GROUP * m
                 before = jnp.maximum(start - 1, 0)
                 previous = jnp.where(start == 0, -1, meta_s[before >> 7, before & 127] >> 9)
                 rows, keeps, rights = [], [], []
@@ -392,7 +375,8 @@
                         j = cols_s[(code >> 7) & 3, i] & 255
                         rights.append(
                             jnp.dot(
-                                a_buf[code & 511], table[j], preferred_element_type=F32
+                                a_buf[code & 511], col_p[j >> 4, (j >> 1) & 7],
+                                preferred_element_type=F32,
                             ).astype(BF)
                         )
                         products[n] = rights[g]
@@ -405,21 +389,25 @@
                 total = running[...]
                 for g in range(GROUP):
                     total = pieces[g] + jnp.where(keeps[g], total, 0.0)
-                    seq[start + g] = total.astype(BF)
+                    seq[start + g] = total
                 running[...] = total
 
             @pl.loop(0, ROWS, unroll=4)
             def _(d):
-                for h in range(2):
-                    key = 64 * q + 32 * h + 2 * d
-                    one = jnp.clip(meta_s[4 + (key >> 7), key & 127], 0, TILES)
-                    two = jnp.clip(meta_s[4 + (key >> 7), (key & 127) + 1], 0, TILES)
-                    parts[d, u, 2 * q + h] = jnp.where(lane[:32] == 0, seq[one], seq[two])
+                for h in range(width):
+                    key = 64 * (width * q + h) + 4 * d
+                    even, even_far, odd_far, odd = [
+                        seq[jnp.clip(meta_s[4 + (key >> 7), (key & 127) + c], 0, TILES)]
+                        for c in range(4)
+                    ]
+                    near = jnp.where(lane[:32] == 0, even, odd)
+                    far = jnp.where(lane[:32] == 0, odd_far, even_far)
+                    parts[d, u, width * q + h] = (near + pltpu.roll(far, 64, 1)).astype(BF)
 
             for there in peers:
-                exchange_copy(there, u, q).start()
-
-    chunks(0, 0, 1)
+                exchange_copy(there, u, pl.ds(width * q, width)).start()
+
+    chunks(0, 0, 2, 1)
     row_arrived(1, held)
     row_send(1, held, right_x)
     row_send(1, held, left_x)
@@ -479,17 +467,16 @@
             pltpu.VMEM((4, 128), I32),
             pltpu.SMEM((4, 128), I32),
             pltpu.VMEM((ROWS, 8, 128), I32),
-            pltpu.VMEM((512, 128), BF),
+            pltpu.VMEM((8, 64, 128), BF),
             pltpu.VMEM((2, 256, 128), BF),
-            pltpu.VMEM((ROWS, 512, 128), BF),
+            pltpu.VMEM((ROWS, 8, 64, 128), BF),
             pltpu.VMEM((2, 8, 256, 128), BF),
             pltpu.VMEM((4, 64, 64, 128), BF),
             pltpu.VMEM((128 * PITCH, 128), F32),
             pltpu.VMEM((TILES, 64, 64), BF),
-            pltpu.VMEM((256, 64, 128), BF),
             pltpu.VMEM((2, 128, 32, 64), BF),
             pltpu.VMEM((TILES, 64, 128), BF),
-            pltpu.VMEM((TILES + 1, 32, 128), BF),
+            pltpu.VMEM((TILES + 1, 32, 128), F32),
             pltpu.VMEM((32, 128), F32),
             pltpu.VMEM((ROWS, 2, 16, 32, 128), BF),
             pltpu.VMEM((16, 128), I32),

time: 86.7 us -> 84.8 us (0.978)
  Pallas kernels: 86.6 us -> 84.7 us
    pallas_call x1, Pallas kernels: 82.1 us -> 80.2 us  [fused(): pl.pallas_call(fused_kernel, out_shape=(jax.ShapeDtypeStruct((ROWS, 2, 16...]
where the time goes in v2:
time: 84.8 us; the launch traced here: 84.7 us
  Pallas kernels  84.7 us (100%)
    pallas_call x1, Pallas kernels, fused(): pl.pallas_call(fused_kernel, out_shape=(jax.ShapeDtypeStruct((ROWS, 2, 16...  80.2 us
    pallas_call x1, Pallas kernels, widen(): pl.pallas_call(widen_kernel, out_shape=jax.ShapeDtypeStruct((256, 64, 128...  4.49 us

profile of v2, /device:TPU:1, one launch (start us, length us, event | category | flops | bytes accessed | tf_op | source)
XLA Modules:
  0.0 84.7 jit_solution(10648612169750284292)
XLA Ops:
  0.0 80.2 %shard_map.46 = (bf16[16,2,16,32,128]{4,3,2,1,0:T(8,128)(2,1)}, s32[16,128]{1,0:T(8,128)}) custom-call(bf16[16,64,64]{2,1,0:T(8,128)(2,1)} %p_hbm.1, s32[1,16]{1,0:T(1,128)} %s_hbm.1, s32[4,128]{1,0:T(4,128)} %bitcast.3, bf16[4,64,64,128]{3,2,1,0:T(8,128)(2,1)} %bitcast.2), custom_call_target="tpu_custom_call" | custom-call | tf_op jit(solution)/shard_map/pallas_call | solution.py:456
  80.2 4.5 %shard_map.47 = f32[256,64,128]{2,1,0:T(8,128)} custom-call(s32[16,128]{1,0:T(8,128)} %get-tuple-element.7.ranks_hbm, bf16[16,2,16,32,128]{4,3,2,1,0:T(8,128)(2,1)} %get-tuple-element.8.got), custom_call_target="tpu_custom_call" | custom-call | tf_op jit(solution)/shard_map/pallas_call | solution.py:533

commit v3 on v2

--- a/solution.py
+++ b/solution.py
@@ -11,7 +11,7 @@
 MIB = 1 << 20
 PITCH = 136
 TILES = 512
-GROUP = 16
+GROUP = 32
 BF = jnp.bfloat16
 F32 = jnp.float32
 I32 = jnp.int32
@@ -259,8 +259,8 @@
             for n in range(4):
                 left[u, 16 * slot + 4 * k + n] = turned[32 * n:32 * n + 32]
 
-    turn(0)
-    turn(1)
+    for k in range(8):
+        turn(k)
 
     row_arrived(0, held)
     row_send(0, held, right_x)
@@ -272,30 +272,6 @@
     col_send(other, left_y)
     col_send(other, sibling)
 
-    before_x, after_x = (x + 3) % 4, (x + 1) % 4
-    before_y, after_y = (y + 3) % 4, (y + 1) % 4
-    row_arrived(0, across_held)
-    row_send(0, across_held, right_x)
-    row_send(0, across_held, left_x)
-
-    def row_relay(u, h):
-        for where, half, there in ((before_x, 0, right_x), (after_x, 1, left_x)):
-            row_arrived(u, slot_at(where, h))
-            row_send(u, slot_at(where, h), there, half)
-
-    def col_relay(a):
-        for where, half, there in ((before_y, 0, right_y), (after_y, 1, left_y)):
-            index = row_of(a, where, core)
-            arrived(col_p.at[index], col_sem.at[index])
-            col_send(index, there, half)
-            col_send(index, sibling)
-
-    for k in range(2, 6):
-        turn(k)
-    row_relay(0, zh)
-    col_relay(zl)
-    turn(6)
-    turn(7)
     inputs[2].wait()
     inputs[3].wait()
     pltpu.make_async_copy(sizes.at[pl.ds(0, 15)], sizes.at[pl.ds(0, 15)], size_sem).wait()
@@ -315,11 +291,31 @@
     to_scalars = pltpu.make_async_copy(meta_v, meta_s, meta_sem)
     to_scalars.start()
 
+    before_x, after_x = (x + 3) % 4, (x + 1) % 4
+    before_y, after_y = (y + 3) % 4, (y + 1) % 4
+    row_arrived(0, across_held)
+    row_send(0, across_held, right_x)
+    row_send(0, across_held, left_x)
+
+    def row_relay(u, h):
+        for where, half, there in ((before_x, 0, right_x), (after_x, 1, left_x)):
+            row_arrived(u, slot_at(where, h))
+            row_send(u, slot_at(where, h), there, half)
+
+    def col_relay(a):
+        for where, half, there in ((before_y, 0, right_y), (after_y, 1, left_y)):
+            index = row_of(a, where, core)
+            arrived(col_p.at[index], col_sem.at[index])
+            col_send(index, there, half)
+            col_send(index, sibling)
+
+    row_relay(0, zh)
+    col_relay(zl)
+    pick(0)
+    pick(1)
     row_relay(0, 1 - zh)
     col_relay(1 - zl)
     first_step(1)
-    pick(0)
-    pick(1)
     for a in (zl, 1 - zl):
         index = row_of(a, (y + 2) % 4, core)
         arrived(col_p.at[index], col_sem.at[index])

time: 84.8 us -> 82.6 us (0.974)
  Pallas kernels: 84.7 us -> 82.5 us
    pallas_call x1, Pallas kernels: 80.2 us -> 78 us  [fused(): pl.pallas_call(fused_kernel, out_shape=(jax.ShapeDtypeStruct((ROWS, 2, 16...]
where the time goes in v3:
time: 82.6 us; the launch traced here: 82.5 us
  Pallas kernels  82.5 us (100%)
    pallas_call x1, Pallas kernels, fused(): pl.pallas_call(fused_kernel, out_shape=(jax.ShapeDtypeStruct((ROWS, 2, 16...  78 us
    pallas_call x1, Pallas kernels, widen(): pl.pallas_call(widen_kernel, out_shape=jax.ShapeDtypeStruct((256, 64, 128...  4.49 us

profile of v3, /device:TPU:1, one launch (start us, length us, event | category | flops | bytes accessed | tf_op | source)
XLA Modules:
  0.0 82.5 jit_solution(5448849297389471495)
XLA Ops:
  0.0 78.0 %shard_map.46 = (bf16[16,2,16,32,128]{4,3,2,1,0:T(8,128)(2,1)}, s32[16,128]{1,0:T(8,128)}) custom-call(bf16[16,64,64]{2,1,0:T(8,128)(2,1)} %p_hbm.1, s32[1,16]{1,0:T(1,128)} %s_hbm.1, s32[4,128]{1,0:T(4,128)} %bitcast.3, bf16[4,64,64,128]{3,2,1,0:T(8,128)(2,1)} %bitcast.2), custom_call_target="tpu_custom_call" | custom-call | tf_op jit(solution)/shard_map/pallas_call | solution.py:452
  78.0 4.5 %shard_map.47 = f32[256,64,128]{2,1,0:T(8,128)} custom-call(s32[16,128]{1,0:T(8,128)} %get-tuple-element.7.ranks_hbm, bf16[16,2,16,32,128]{4,3,2,1,0:T(8,128)(2,1)} %get-tuple-element.8.got), custom_call_target="tpu_custom_call" | custom-call | tf_op jit(solution)/shard_map/pallas_call | solution.py:529

commit v4 on v3

--- a/solution.py
+++ b/solution.py
@@ -315,11 +315,11 @@
     pick(1)
     row_relay(0, 1 - zh)
     col_relay(1 - zl)
-    first_step(1)
     for a in (zl, 1 - zl):
         index = row_of(a, (y + 2) % 4, core)
         arrived(col_p.at[index], col_sem.at[index])
         col_send(index, sibling)
+    first_step(1)
     pick(2)
     pick(3)
     to_scalars.wait()

time: 82.6 us -> 82.8 us (level)
  no operation moved by 1% of the time
where the time goes in v4:
time: 82.8 us; the launch traced here: 82.7 us
  Pallas kernels  82.7 us (100%)
    pallas_call x1, Pallas kernels, fused(): pl.pallas_call(fused_kernel, out_shape=(jax.ShapeDtypeStruct((ROWS, 2, 16...  78.2 us
    pallas_call x1, Pallas kernels, widen(): pl.pallas_call(widen_kernel, out_shape=jax.ShapeDtypeStruct((256, 64, 128...  4.49 us

profile of v4, /device:TPU:1, one launch (start us, length us, event | category | flops | bytes accessed | tf_op | source)
XLA Modules:
  0.0 82.7 jit_solution(7375143090035590731)
XLA Ops:
  0.0 78.2 %shard_map.46 = (bf16[16,2,16,32,128]{4,3,2,1,0:T(8,128)(2,1)}, s32[16,128]{1,0:T(8,128)}) custom-call(bf16[16,64,64]{2,1,0:T(8,128)(2,1)} %p_hbm.1, s32[1,16]{1,0:T(1,128)} %s_hbm.1, s32[4,128]{1,0:T(4,128)} %bitcast.3, bf16[4,64,64,128]{3,2,1,0:T(8,128)(2,1)} %bitcast.2), custom_call_target="tpu_custom_call" | custom-call | tf_op jit(solution)/shard_map/pallas_call | solution.py:452
  78.2 4.5 %shard_map.47 = f32[256,64,128]{2,1,0:T(8,128)} custom-call(s32[16,128]{1,0:T(8,128)} %get-tuple-element.7.ranks_hbm, bf16[16,2,16,32,128]{4,3,2,1,0:T(8,128)(2,1)} %get-tuple-element.8.got), custom_call_target="tpu_custom_call" | custom-call | tf_op jit(solution)/shard_map/pallas_call | solution.py:529
